TPU v7x, 1024 devices: a whole 4x8x16 slice. The times are simulated.
1024 devices in a mesh: dp: 32 (over y, x_hi, core), expert: 32 (over x_lo, z).
Axes of the slice: x: 4 (x_hi: 2, x_lo: 2; x = x_hi * 2 + x_lo), y: 8, z: 16, core: 2. Of those that a mesh axis runs over, the one named last changes fastest.
Arguments:
- cotangent: bfloat16 [131072, 3584], P(('dp', 'expert')), may hold values from -6 to 6
- gates: bfloat16 [131072, 1], P(('dp', 'expert')), may hold values from 0.049804688 to 1
- expert_ids: int32 [131072, 1], P(('dp', 'expert')), may hold values from 0 to 63; in each aligned block of 128 rows (0 to 127, 128 to 255, ...) at most 3 rows name the same one
- hidden: bfloat16 [32, 64, 32, 3, 2560], P('dp', 'expert'), may hold values from -6 to 6
- factor_a: bfloat16 [64, 2560, 128], P('expert'), may hold values from -0.125 to 0.125
- factor_b: bfloat16 [64, 128, 3584], P('expert'), may hold values from -0.5 to 0.5
Outputs:
- grad_a: float32 [64, 2560, 128], P('expert', 'dp')
- grad_b: float32 [64, 128, 3584], P('expert', None, 'dp')
- grad_hidden: bfloat16 [32, 64, 32, 3, 2560], P('dp', 'expert')
- grad_gates: float32 [131072, 1], P(('dp', 'expert'))
Inputs may be any that keep to these rules, and one draw needn't show every extreme that they name: `expert_ids`: among the 128 tokens of one device no expert is named more than 3 times, a bound that some block reaches.
All inputs are finite; a program needn't handle non-finite values.
Results may differ from a plain program's by a relative error of at most 0.0057.
Values may be sent and summed in bfloat16 or wider, within the bound.
No kernel may reach another device: no remote copies, remote signals or barrier semaphores. Data moves between devices by JAX's collectives and lax.ppermute only.
A program may use at most 64 MiB of HBM per device.

v0:
```python
import jax
import jax.numpy as jnp
from jax import lax
from jax.sharding import PartitionSpec as P


def body(cotangent, gates, expert_ids, hidden, factor_a, factor_b):
    tok_count = cotangent.shape[0]
    top_count = expert_ids.shape[1]
    width = cotangent.shape[1]
    groups = lax.axis_size("expert")
    local_experts = factor_a.shape[0]
    experts_all = groups * local_experts
    slots_per = hidden.shape[3]
    pair_count = tok_count * top_count
    slot_count = experts_all * slots_per
    flat_ids = expert_ids.reshape(pair_count)
    onehot = (flat_ids[:, None] == jnp.arange(experts_all, dtype=jnp.int32)[None, :]).astype(
        jnp.float32
    )
    order_idx = jnp.arange(pair_count, dtype=jnp.int32)
    earlier = (order_idx[:, None] > order_idx[None, :]).astype(jnp.float32)
    before = jnp.dot(earlier, onehot, preferred_element_type=jnp.float32)
    rank = jnp.sum(before * onehot, axis=1).astype(jnp.int32)
    slot_of = flat_ids * slots_per + rank
    placing = (slot_of[:, None] == jnp.arange(slot_count, dtype=jnp.int32)[None, :]).astype(
        jnp.float32
    )
    token_place = jnp.sum(placing.reshape(tok_count, top_count, slot_count), axis=1).astype(
        jnp.bfloat16
    )
    send_rows = lax.dot_general(
        token_place, cotangent, (((0,), (0,)), ((), ())), preferred_element_type=jnp.float32
    )
    send_rows = send_rows.astype(jnp.bfloat16).reshape(groups, local_experts, slots_per, width)
    send_gate = jnp.dot(
        gates.reshape(pair_count).astype(jnp.float32), placing, precision=lax.Precision.HIGHEST
    )
    send_gate = send_gate.astype(jnp.bfloat16).reshape(groups, local_experts, slots_per)
    got_rows, got_gate = (
        lax.all_to_all(send_rows, "expert", split_axis=0, concat_axis=0, tiled=True),
        lax.all_to_all(send_gate, "expert", split_axis=0, concat_axis=0, tiled=True),
    )
    slot_output_gradient = (
        got_gate.astype(jnp.float32)[:, :, :, None] * got_rows.astype(jnp.float32)
    ).astype(jnp.bfloat16)
    saved = hidden[0]
    low = jnp.einsum("lscf,lfr->lscr", saved, factor_a, preferred_element_type=jnp.float32).astype(
        jnp.bfloat16
    )
    grad_low = jnp.einsum(
        "slcd,lrd->lscr", slot_output_gradient, factor_b, preferred_element_type=jnp.float32
    ).astype(jnp.bfloat16)
    part_b = jnp.einsum(
        "lscr,slcd->lrd", low, slot_output_gradient, preferred_element_type=jnp.float32
    )
    slot_out = jnp.einsum("lscr,lrd->slcd", low, factor_b, preferred_element_type=jnp.float32)
    slot_gate = jnp.sum(got_rows.astype(jnp.float32) * slot_out, axis=3)
    back = lax.all_to_all(slot_gate, "expert", split_axis=0, concat_axis=0, tiled=True)
    grad_gates = jnp.dot(
        placing, back.reshape(slot_count), precision=lax.Precision.HIGHEST
    ).reshape(tok_count, top_count)
    grad_hidden = jnp.einsum(
        "lscr,lfr->lscf", grad_low, factor_a, preferred_element_type=jnp.float32
    ).astype(jnp.bfloat16)
    part_a = jnp.einsum("lscf,lscr->lfr", saved, grad_low, preferred_element_type=jnp.float32)
    grad_a, grad_b = (
        lax.psum_scatter(part_a, "dp", scatter_dimension=1, tiled=True),
        lax.psum_scatter(part_b, "dp", scatter_dimension=2, tiled=True),
    )
    return (grad_a, grad_b, grad_hidden[None], grad_gates)


def solution(mesh):
    placed = (
        P(("dp", "expert"), None),
        P(("dp", "expert"), None),
        P(("dp", "expert"), None),
        P("dp", "expert", None, None, None),
        P("expert", None, None),
        P("expert", None, None),
    )
    return jax.shard_map(
        body,
        mesh=mesh,
        in_specs=placed,
        out_specs=(
            P("expert", "dp", None),
            P("expert", None, "dp"),
            P("dp", "expert", None, None, None),
            P(("dp", "expert"), None),
        ),
        check_vma=False,
    )
```

profile of v0, /device:TPU:1, one launch (start us, length us, event | category | flops | bytes accessed | tf_op | source)
XLA Modules:
  0.0 571.3 jit_solution(8799438052058609003)
XLA Ops:
  7.2 0.0 copy-start
  7.2 1.0 fusion.18
  8.2 0.7 fusion.28
  8.8 0.9 fusion.23
  9.7 0.8 reshape.46
  10.5 20.6 %all-to-all-start = ((bf16[32,2,3]{2,1,0:T(2,128)(2,1)}), bf16[32,2,3]{2,1,0:T(2,128)(2,1)S(1)}, u32[]{:S(2)}, u32[]{:S(2)}) async-start(bf16[32,2,3]{2,1,0:T(2,128)(2,1)} %reshape.46), calls=%async_computation | async-start | bytes 32768 | tf_op jit(solution)/shard_map/all_to_all | solution.py:42
  31.1 1.8 convolution_convert_fusion
  32.9 2.2 reshape.47
  35.0 3.8 copy.43
  38.8 4.4 all-to-all-done
  43.2 8.2 %all-to-all-start.1 = ((bf16[32,2,3,3584]{3,1,2,0:T(2,128)(2,1)}), bf16[32,2,3,3584]{3,1,2,0:T(2,128)(2,1)S(1)}, u32[]{:S(2)}, u32[]{:S(2)}) async-start(bf16[32,2,3,3584]{3,1,2,0:T(2,128)(2,1)} %copy.43), calls=%async_computation.1 | async-start | bytes 2752512 | tf_op jit(solution)/shard_map/all_to_all | solution.py:41
  51.4 0.0 all-reduce.3.cloned.1.call-start
  51.4 0.1 copy.41
  51.5 61.2 %all-to-all-done.1 = bf16[32,2,3,3584]{3,1,2,0:T(2,128)(2,1)S(1)} async-done(((bf16[32,2,3,3584]{3,1,2,0:T(2,128)(2,1)}), bf16[32,2,3,3584]{3,1,2,0:T(2,128)(2,1)S(1)}, u32[]{:S(2)}, u32[]{:S(2)}) %all-to-all-start.1) | async-done | bytes 1376288 | tf_op jit(solution)/shard_map/all_to_all | solution.py:41
  112.8 0.0 copy-done
  112.8 0.0 copy-start.1
  112.8 0.8 fusion.15
  113.5 0.4 copy-done.1
  114.0 2.1 convolution_bitcast_fusion.2
  116.0 5.1 copy.45
  121.1 0.0 all-reduce.3.cloned.1.call-update
  121.2 0.0 reduce-scatter.2.cloned.1.call-start
  121.2 2.0 fusion.12
  123.3 2.7 convolution_bitcast_fusion
  125.9 0.0 reduce-scatter.2.cloned.1.call-update
  126.0 1.3 dynamic-slice
  127.9 0.6 fusion.6
  128.5 0.7 copy.46
  129.2 11.5 %all-to-all-start.2 = ((f32[32,2,3]{2,1,0:T(2,128)}), f32[32,2,3]{2,1,0:T(2,128)S(1)}, u32[]{:S(2)}, u32[]{:S(2)}) async-start(f32[32,2,3]{2,1,0:T(2,128)} %copy.46), calls=%async_computation.3 | async-start | bytes 65536 | tf_op jit(solution)/shard_map/all_to_all | solution.py:59
  140.7 2.8 fusion.1
  143.5 9.7 %all-to-all-done.2 = f32[32,2,3]{2,1,0:T(2,128)S(1)} async-done(((f32[32,2,3]{2,1,0:T(2,128)}), f32[32,2,3]{2,1,0:T(2,128)S(1)}, u32[]{:S(2)}, u32[]{:S(2)}) %all-to-all-start.2) | async-done | bytes 800 | tf_op jit(solution)/shard_map/all_to_all | solution.py:59
  153.2 0.1 reshape.56
  153.4 0.8 convolution_bitcast_fusion.3
  154.2 259.4 %all-reduce.3.cloned.1.call-done = f32[2,2560,128]{2,0,1:T(2,128)} async-done(((f32[2,2560,128]{2,0,1:T(2,128)}), f32[2,2560,128]{2,0,1:T(2,128)}) %all-reduce.3.cloned.1.call-update) | async-done | bytes 2621456
  413.6 0.9 constant_dynamic-slice_fusion
  414.4 0.6 copy.47
  415.1 149.4 %reduce-scatter.2.cloned.1.call-done = f32[2,128,112]{1,2,0:T(8,128)} async-done(((f32[2,128,3584]{1,2,0:T(8,128)}), f32[2,128,112]{1,2,0:T(8,128)}) %reduce-scatter.2.cloned.1.call-update) | async-done | bytes 114704 | tf_op jit(solution)/shard_map/reduce_scatter | solution.py:69
  (2 shorter events, 0.0 us)
Async XLA Ops:
  7.2 105.6 %copy-start = (bf16[2,128,3584]{2,1,0:T(8,128)(2,1)S(1)}, bf16[2,128,3584]{2,1,0:T(8,128)(2,1)}, u32[]{:S(2)}) copy-start(bf16[2,128,3584]{2,1,0:T(8,128)(2,1)} %param.11) | copy-start | bytes 5505028
  10.5 32.7 %all-to-all-start = ((bf16[32,2,3]{2,1,0:T(2,128)(2,1)}), bf16[32,2,3]{2,1,0:T(2,128)(2,1)S(1)}, u32[]{:S(2)}, u32[]{:S(2)}) async-start(bf16[32,2,3]{2,1,0:T(2,128)(2,1)} %reshape.46), calls=%async_computation | async-start | bytes 32768 | tf_op jit(solution)/shard_map/all_to_all | solution.py:42
  43.2 69.6 %all-to-all-start.1 = ((bf16[32,2,3,3584]{3,1,2,0:T(2,128)(2,1)}), bf16[32,2,3,3584]{3,1,2,0:T(2,128)(2,1)S(1)}, u32[]{:S(2)}, u32[]{:S(2)}) async-start(bf16[32,2,3,3584]{3,1,2,0:T(2,128)(2,1)} %copy.43), calls=%async_computation.1 | async-start | bytes 2752512 | tf_op jit(solution)/shard_map/all_to_all | solution.py:41
  51.4 362.2 %all-reduce.3.cloned.1.call-start = ((), (), s32[]{:S(2)}) async-start(), calls=%async_computation.5 | async-start | bytes 5242880
  112.8 1.2 copy-start.1
  121.2 443.3 %reduce-scatter.2.cloned.1.call-start = ((), (), s32[]{:S(2)}) async-start(), calls=%async_computation.4 | async-start | bytes 3784704 | tf_op jit(solution)/shard_map/reduce_scatter | solution.py:69
  129.2 24.0 %all-to-all-start.2 = ((f32[32,2,3]{2,1,0:T(2,128)}), f32[32,2,3]{2,1,0:T(2,128)S(1)}, u32[]{:S(2)}, u32[]{:S(2)}) async-start(f32[32,2,3]{2,1,0:T(2,128)} %copy.46), calls=%async_computation.3 | async-start | bytes 65536 | tf_op jit(solution)/shard_map/all_to_all | solution.py:59
Sparse Core Ops, SparseCore 0:
  121.3 292.2 all-reduce.2
  420.1 144.3 reduce-scatter.1
where the time goes:
time: 576 us; the launch traced here: 571 us
  waiting for transfers between devices  484 us (84%)
  starting transfers between devices  40.4 us (7%)
  local copies, waits for them, and re-layouts  16 us (3%)
  matrix products  15.4 us (3%)
  between operations  14.8 us (3%)
    unnamed x3, waiting for transfers between devices  259 us
    reduce_scatter x1, waiting for transfers between devices, body(): lax.psum_scatter(part_b, 'dp', scatter_dimension=2, tiled=True)  149 us
    all_to_all x1, waiting for transfers between devices, body(): lax.all_to_all(send_rows, 'expert', split_axis=0, concat_axis=0, tiled=True)  61.2 us
    all_to_all x1, starting transfers between devices, body(): lax.all_to_all(send_gate, 'expert', split_axis=0, concat_axis=0, tiled=True)  20.6 us
  transfers between devices with their start and end apart: 5, of which 5 were waited for; matrix products, arithmetic and copies ran while one was open for 4% of the time, Pallas kernels for 0%

commit v1 on v0

v1 whole, which is shorter than its diff:
```python
import jax
import jax.numpy as jnp
from jax import lax
from jax.experimental import pallas as pl
from jax.experimental.pallas import tpu as pltpu
from jax.sharding import Mesh, PartitionSpec as P

CAP = 3
ROWS = 4
SIDES = ("k", "expert")
GROUPS = ("q", "k")


def place_kernel(experts, ids_ref, gate_ref, part_ref, last_ref, send_ref, row_ref):
    tokens = ids_ref.shape[1]
    ids = ids_ref[...]
    expert = lax.broadcasted_iota(jnp.int32, (experts, tokens), 0)
    named = expert == ids
    older = lax.broadcasted_iota(jnp.int32, (tokens, tokens), 0)
    newer = lax.broadcasted_iota(jnp.int32, (tokens, tokens), 1)
    before = jnp.dot(
        named.astype(jnp.bfloat16),
        (older < newer).astype(jnp.bfloat16),
        preferred_element_type=jnp.float32,
    )
    rank = jnp.sum(jnp.where(named, before, 0.0), axis=0, keepdims=True).astype(jnp.int32)
    block = (ids % 2) * (experts // 2) + ids // 2
    row_ref[...] = block * ROWS + rank

    c = pl.program_id(0)
    row = lax.broadcasted_iota(jnp.int32, (experts * ROWS, tokens), 0)
    whole = row == block * ROWS + rank
    rest = (row == block * ROWS + CAP) & (rank == c)
    gate = jnp.sum(
        jnp.where(whole | rest, gate_ref[...].astype(jnp.float32), 0.0), axis=1, keepdims=True
    )
    rows = jnp.dot(
        whole.astype(jnp.bfloat16), part_ref[...], preferred_element_type=jnp.float32
    ) + jnp.dot(rest.astype(jnp.bfloat16), last_ref[...], preferred_element_type=jnp.float32)
    out = (rows * gate).astype(jnp.bfloat16)
    send_ref[...] = out.reshape(send_ref.shape)


def place(ids, gates, cotangent, experts):
    tokens, width = cotangent.shape
    quarter = width // ROWS
    return pl.pallas_call(
        lambda *refs: place_kernel(experts, *refs),
        grid=(CAP,),
        in_specs=[
            pl.BlockSpec((1, tokens), lambda c: (0, 0)),
            pl.BlockSpec((1, tokens), lambda c: (0, 0)),
            pl.BlockSpec((tokens, quarter), lambda c: (0, c)),
            pl.BlockSpec((tokens, quarter), lambda c: (0, CAP)),
        ],
        out_specs=[
            pl.BlockSpec((experts, ROWS, quarter), lambda c: (0, 0, c)),
            pl.BlockSpec((1, tokens), lambda c: (0, 0)),
        ],
        out_shape=[
            jax.ShapeDtypeStruct((experts, ROWS, CAP * quarter), jnp.bfloat16),
            jax.ShapeDtypeStruct((1, tokens), jnp.int32),
        ],
        name="place_rows",
    )(ids, gates, cotangent, cotangent)


def grads_kernel(got_ref, b_ref, low_ref, rest_ref, back_ref, hidden_ref, out_ref, gl_ref, sg_ref):
    slots, rank = low_ref.shape
    quarter = b_ref.shape[1] // ROWS
    across = (((1,), (1,)), ((), ()))
    down = (((0,), (0,)), ((), ()))
    place_in = lax.broadcasted_iota(jnp.int32, (slots, rank), 0) % ROWS
    low = low_ref[...]
    total = jnp.zeros((slots, rank), jnp.float32)
    last = jnp.zeros((quarter, rank), jnp.float32)
    cut = out_ref.shape[0]
    a_rows = hidden_ref.shape[1] // cut
    b_rows = b_ref.shape[1] // cut
    per = cut // ROWS
    for c in range(CAP):
        x = got_ref[:, :, c * quarter : (c + 1) * quarter].reshape(slots, quarter)
        main = lax.dot_general(
            x, b_ref[:, c * quarter : (c + 1) * quarter], across, preferred_element_type=jnp.float32
        )
        rest = lax.dot_general(
            x, b_ref[:, CAP * quarter :], across, preferred_element_type=jnp.float32
        )
        total = total + jnp.where(place_in < CAP, main, 0.0)
        rest = jnp.concatenate([rest[CAP - c :], rest[: CAP - c]], axis=0)
        total = total + jnp.where(place_in == c, rest, 0.0)
        both = lax.dot_general(
            x,
            jnp.concatenate([low, rest_ref[c]], axis=1),
            down,
            preferred_element_type=jnp.float32,
        )
        last = last + both[:, rank:]
        out_ref[c * per : (c + 1) * per, a_rows:, :] = (
            both[:, :rank].astype(jnp.bfloat16).reshape(per, b_rows, rank)
        )
    out_ref[CAP * per :, a_rows:, :] = last.astype(jnp.bfloat16).reshape(per, b_rows, rank)
    sg = jnp.sum(total * low.astype(jnp.float32), axis=1, keepdims=True)
    sg_ref[...] = jnp.broadcast_to(sg, (slots, rank))
    grad_low = jnp.dot(
        back_ref[...], total.astype(jnp.bfloat16), preferred_element_type=jnp.float32
    ).astype(jnp.bfloat16)
    gl_ref[...] = grad_low
    out_ref[:, :a_rows, :] = (
        lax.dot_general(hidden_ref[...], grad_low, down, preferred_element_type=jnp.float32)
        .astype(jnp.bfloat16)
        .reshape(cut, a_rows, rank)
    )


def slot_grads(got, b, low, rest, back, hidden, cut):
    slots, rank = low.shape
    rows = (hidden.shape[1] + b.shape[1]) // cut
    return pl.pallas_call(
        grads_kernel,
        out_shape=[
            jax.ShapeDtypeStruct((cut, rows, rank), jnp.bfloat16),
            jax.ShapeDtypeStruct((hidden.shape[0], rank), jnp.bfloat16),
            jax.ShapeDtypeStruct((slots, rank), jnp.float32),
        ],
        compiler_params=pltpu.CompilerParams(vmem_limit_bytes=48 * 2**20),
        name="slot_grads",
    )(got, b, low, rest, back, hidden)


def body(cotangent, gates, expert_ids, hidden, factor_a, factor_b):
    tokens = cotangent.shape[0]
    sources = lax.axis_size("expert")
    experts = 2 * sources
    groups = 2 * lax.axis_size("q")
    core = lax.axis_index("k")
    me = core * sources + lax.axis_index("expert")
    units, rank = factor_a.shape[1], factor_a.shape[2]
    width = factor_b.shape[2]
    a_rows = units // groups
    pair = [(0, 1), (1, 0)]

    send, row = place(expert_ids.reshape(1, tokens), gates.reshape(1, tokens), cotangent, experts)
    got = lax.all_to_all(send, SIDES, split_axis=0, concat_axis=0, tiled=True)

    saved = jnp.transpose(hidden[0], (0, 2, 1, 3)).reshape(2, CAP * sources, units)
    own = lax.dynamic_index_in_dim(saved, core, 0, keepdims=False)
    other = lax.ppermute(
        lax.dynamic_index_in_dim(saved, 1 - core, 0, keepdims=False), "k", pair
    )
    mine = jnp.where(core == 0, jnp.stack([own, other]), jnp.stack([other, own]))
    a_mine = lax.dynamic_index_in_dim(factor_a, core, 0, keepdims=False)
    b_mine = lax.dynamic_index_in_dim(factor_b, core, 0, keepdims=False)
    low = jnp.einsum("gsf,fr->gsr", mine, a_mine, preferred_element_type=jnp.float32).astype(
        jnp.bfloat16
    )
    low = low.reshape(2, CAP, sources, rank)
    by_source = jnp.transpose(low, (0, 2, 1, 3)).reshape(experts, CAP, rank)
    whole = jnp.pad(by_source, ((0, 0), (0, 1), (0, 0))).reshape(experts * ROWS, rank)
    rest = jnp.pad(
        jnp.transpose(by_source, (1, 0, 2))[:, :, None, :], ((0, 0), (0, 0), (CAP, 0), (0, 0))
    ).reshape(CAP, experts * ROWS, rank)
    slot = jnp.arange(experts * CAP, dtype=jnp.int32)
    group, place_c, source = slot // (CAP * sources), slot // sources % CAP, slot % sources
    at_row = (group * sources + source) * ROWS + place_c
    back_rows = (
        at_row[:, None] == jnp.arange(experts * ROWS, dtype=jnp.int32)[None, :]
    ).astype(jnp.bfloat16)

    parts, grad_low, slot_gate = slot_grads(
        got, b_mine, whole, rest, back_rows, mine.reshape(2 * CAP * sources, units), groups
    )
    summed = lax.all_to_all(parts, GROUPS, split_axis=0, concat_axis=0, tiled=True)
    summed = jnp.sum(
        summed.reshape(groups // 2, 2, *summed.shape[1:]).astype(jnp.float32), axis=0
    )
    grad_a = summed[:, :a_rows]
    grad_b = jnp.transpose(summed[:, a_rows:], (0, 2, 1))

    grad_low = grad_low.reshape(2, CAP * sources, rank)
    kept = lax.dynamic_index_in_dim(grad_low, core, 0, keepdims=False)
    sent = lax.ppermute(
        lax.dynamic_index_in_dim(grad_low, 1 - core, 0, keepdims=False), "k", pair
    )
    grad_low = jnp.where(core == 0, jnp.stack([kept, sent]), jnp.stack([sent, kept]))
    grad_hidden = jnp.einsum(
        "lsr,lfr->lsf", grad_low, factor_a, preferred_element_type=jnp.float32
    ).astype(jnp.bfloat16)
    grad_hidden = jnp.transpose(grad_hidden.reshape(2, CAP, sources, units), (0, 2, 1, 3))

    slot_gate = slot_gate[:, 0].reshape(experts, ROWS)
    away = jnp.arange(experts, dtype=jnp.int32) ^ me
    pick = (away[:, None] == jnp.arange(experts, dtype=jnp.int32)[None, :]).astype(jnp.float32)
    home = jnp.dot(pick, slot_gate, precision=lax.Precision.HIGHEST)
    bit = 1
    while bit < experts:
        home = home.reshape(experts // (2 * bit), 2, bit, ROWS)
        if bit < sources:
            there = [(i, i ^ bit) for i in range(sources)]
            moved = lax.ppermute(home[:, 1], "expert", there)
        else:
            moved = lax.ppermute(home[:, 1], "k", pair)
        home = jnp.stack([home[:, 0], moved], axis=1)
        bit *= 2
    row = row.reshape(tokens)
    row = ((row // ROWS) ^ me) * ROWS + row % ROWS
    chosen = (row[:, None] == jnp.arange(experts * ROWS, dtype=jnp.int32)[None, :]).astype(
        jnp.float32
    )
    grad_gates = jnp.dot(
        chosen, home.reshape(experts * ROWS, 1), precision=lax.Precision.HIGHEST
    ) / gates.astype(jnp.float32)
    return grad_a, grad_b, grad_hidden[None], grad_gates


def solution(mesh):
    fine = Mesh(
        mesh.devices.reshape(mesh.shape["dp"] // 2, 2, mesh.shape["expert"]),
        ("q", "k", "expert"),
    )
    dp = GROUPS
    tokens = P(("q", "k", "expert"), None)
    return jax.shard_map(
        body,
        mesh=fine,
        in_specs=(
            tokens,
            tokens,
            tokens,
            P(dp, "expert", None, None, None),
            P("expert", None, None),
            P("expert", None, None),
        ),
        out_specs=(
            P("expert", dp, None),
            P("expert", None, dp),
            P(dp, "expert", None, None, None),
            tokens,
        ),
        check_vma=False,
    )
```

time: 576 us -> 164 us (0.28)
  waiting for transfers between devices: 484 us -> 81 us
  starting transfers between devices: 40.4 us -> 60.8 us
  between operations: 14.8 us -> 0.93 us
  matrix products: 15.4 us -> 2.88 us
  local copies, waits for them, and re-layouts: 16 us -> 8.23 us
  Pallas kernels: 0 us -> 7.48 us
    unnamed x3 -> x0, waiting for transfers between devices: 259 us -> none
    reduce_scatter x1 -> x0, waiting for transfers between devices: 149 us -> none  [body(): lax.psum_scatter(part_b, 'dp', scatter_dimension=2, tiled=True)]
    ppermute x0 -> x8, starting transfers between devices: none -> 27.4 us  [the longest x5 16.4 us: body(): moved = lax.ppermute(home[:, 1], 'expert', there)]
    ppermute x0 -> x8, waiting for transfers between devices: none -> 20.6 us  [the longest x5 19.9 us: body(): moved = lax.ppermute(home[:, 1], 'expert', there)]
    all_to_all x3 -> x2, waiting for transfers between devices: 75.3 us -> 60.4 us  [the longest x1 60.4 us: body(): got = lax.all_to_all(send, SIDES, split_axis=0, concat_axis=0, tiled=True)]
    dot_general x10 -> x4, matrix products: 15.4 us -> 2.88 us  [the longest x1 1.5 us: body(): jnp.einsum('lsr,lfr->lsf', grad_low, factor_a, preferred_element_type=jnp...]
    pallas_call x0 -> x2, Pallas kernels: none -> 7.48 us  [the longest x1 4.27 us: place(): pl.pallas_call(lambda *refs: place_kernel(experts, *refs), grid=(CAP,), i...]
    all_to_all x3 -> x2, starting transfers between devices: 40.3 us -> 33.4 us  [the longest x1 22.1 us: body(): got = lax.all_to_all(send, SIDES, split_axis=0, concat_axis=0, tiled=True)]
  transfers between devices with their start and end apart: 5 -> 10, of which waited for: 5 -> 8; matrix products, arithmetic and copies ran while one was open for 4% -> 4% of each run, Pallas kernels for 0% -> 0%
where the time goes in v1:
time: 164 us; the launch traced here: 163 us
  waiting for transfers between devices  81 us (49%)
  starting transfers between devices  60.8 us (37%)
  local copies, waits for them, and re-layouts  8.23 us (5%)
  Pallas kernels  7.48 us (5%)
  matrix products  2.88 us (2%)
  other arithmetic  2 us (1%)
    all_to_all x1, waiting for transfers between devices, body(): got = lax.all_to_all(send, SIDES, split_axis=0, concat_axis=0, tiled=True)  60.4 us
    all_to_all x1, starting transfers between devices, body(): got = lax.all_to_all(send, SIDES, split_axis=0, concat_axis=0, tiled=True)  22.1 us
    ppermute x5, waiting for transfers between devices, body(): moved = lax.ppermute(home[:, 1], 'expert', there)  19.9 us
    ppermute x5, starting transfers between devices, body(): moved = lax.ppermute(home[:, 1], 'expert', there)  16.4 us
    all_to_all x1, starting transfers between devices, body(): lax.all_to_all(parts, GROUPS, split_axis=0, concat_axis=0, tiled=True)  11.3 us
    ppermute x1, starting transfers between devices, body(): moved = lax.ppermute(home[:, 1], 'k', pair)  6.75 us
    pallas_call x1, Pallas kernels, place(): pl.pallas_call(lambda *refs: place_kernel(experts, *refs), grid=(CAP,), i...  4.27 us
  transfers between devices with their start and end apart: 10, of which 8 were waited for; matrix products, arithmetic and copies ran while one was open for 4% of the time, Pallas kernels for 0%

profile of v1, /device:TPU:1, one launch (start us, length us, event | category | flops | bytes accessed | tf_op | source)
XLA Modules:
  0.0 163.3 jit_solution(10985545748383427719)
XLA Ops:
  0.6 4.3 %place_rows.1 = (bf16[64,4,2688]{2,1,0:T(4,128)(2,1)}, s32[1,128]{1,0:T(1,128)}) custom-call(s32[1,128]{1,0:T(1,128)} %bitcast.118, bf16[1,128]{1,0:T(2,128)(2,1)} %bitcast.119, bf16[128,3584]{1,0:T(8,128)(2,1)} %refs_3_.1, bf16[128,3584]{1,0:T(8,128)(2,1)} %refs_3_.1), custom_call_target="tpu_custom_call" | custom-call | tf_op jit(solution)/shard_map/place_rows/pallas_call | solution.py:47
  4.9 22.1 %all-to-all-start = ((bf16[64,4,2688]{2,1,0:T(4,128)(2,1)}), bf16[64,4,2688]{2,1,0:T(4,128)(2,1)}, u32[]{:S(2)}, u32[]{:S(2)}) async-start(bf16[64,4,2688]{2,1,0:T(4,128)(2,1)} %get-tuple-element.9), calls=%async_computation | async-start | bytes 2752512 | tf_op jit(solution)/shard_map/all_to_all | solution.py:144
  27.1 1.0 constant_dynamic-slice_fusion.1
  28.1 2.3 %collective-permute-start = (bf16[96,2560]{1,0:T(8,128)(2,1)}, bf16[96,2560]{1,0:T(8,128)(2,1)S(1)}, u32[]{:S(2)}, u32[]{:S(2)}) collective-permute-start(bf16[96,2560]{1,0:T(8,128)(2,1)} %get-tuple-element.15), channel_id=1, source_target_pairs={{0,32},{32,0},{1,33},{33,1},{2,34},{34,2},{3,35},{35,3},{4,36},{36... | collective-permute-start | bytes 1474568 | tf_op jit(solution)/shard_map/ppermute | solution.py:148
  30.5 0.1 fusion.3.back_ref
  30.6 1.0 dynamic-slice_bitcast_fusion.b_ref
  31.6 0.5 collective-permute-done
  32.1 0.2 maximum_select_fusion
  32.3 0.6 copy-done.3
  32.9 0.4 convolution_convert_fusion.1
  33.5 0.1 pad.9.clone
  33.7 60.4 %all-to-all-done.got_ref = bf16[64,4,2688]{2,1,0:T(4,128)(2,1)} async-done(((bf16[64,4,2688]{2,1,0:T(4,128)(2,1)}), bf16[64,4,2688]{2,1,0:T(4,128)(2,1)}, u32[]{:S(2)}, u32[]{:S(2)}) %all-to-all-start) | async-done | bytes 1376288 | tf_op jit(solution)/shard_map/all_to_all | solution.py:144
  94.0 1.2 copy-done.1
  95.2 3.2 %slot_grads.1 = (bf16[32,192,128]{2,1,0:T(8,128)(2,1)S(1)}, bf16[192,128]{1,0:T(8,128)(2,1)S(1)}, f32[256,128]{1,0:T(8,128)S(1)}) custom-call(bf16[64,4,2688]{2,1,0:T(4,128)(2,1)} %all-to-all-done.got_ref, bf16[128,3584]{1,0:T(8,128)(2,1)S(1)} %copy-done.1, bf16[256,128]{1,0:T(8,128)(2,1)S(1)} %bitcast.100, bf16[3,256,128]{2,1,0:T(8,128)(2,1)S(1)} %bitcast.99, ...), custom_call_target="tpu_custom_call" | custom-call | tf_op jit(solution)/shard_map/slot_grads/pallas_call | solution.py:119
  98.4 1.1 copy-done.2
  99.6 11.3 %all-to-all-start.1 = ((bf16[32,192,128]{2,1,0:T(8,128)(2,1)}), bf16[32,192,128]{2,1,0:T(8,128)(2,1)}, u32[]{:S(2)}, u32[]{:S(2)}) async-start(bf16[32,192,128]{2,1,0:T(8,128)(2,1)} %copy-done.2), calls=%async_computation.1 | async-start | bytes 3145728 | tf_op jit(solution)/shard_map/all_to_all | solution.py:173
  110.9 0.1 slice_reduce_fusion
  111.0 0.1 reshape_squeeze.3
  111.1 0.2 convolution_bitcast_fusion
  111.3 3.0 %collective-permute-start.2 = (f32[32,1,4]{0,2,1:T(4,128)S(1)}, f32[32,1,4]{0,2,1:T(4,128)S(1)}, u32[]{:S(2)}, u32[]{:S(2)}) collective-permute-start(f32[32,1,4]{0,2,1:T(4,128)S(1)} %get-tuple-element.29), channel_id=1, source_target_pairs={{0,1},{1,0},{2,3},{3,2},{4,5},{5,4},{6,7},{7,6},{8,9},{9,8},{10,11... | collective-permute-start | bytes 1544 | tf_op jit(solution)/shard_map/ppermute | solution.py:200
  114.4 0.1 copy.39
  114.4 0.1 copy.41
  114.5 1.6 collective-permute-done.2
  116.2 0.1 copy.42
  116.3 3.7 %collective-permute-start.3 = (f32[16,2,4]{0,2,1:T(4,128)S(1)}, f32[16,2,4]{0,2,1:T(4,128)S(1)}, u32[]{:S(2)}, u32[]{:S(2)}) collective-permute-start(f32[16,2,4]{0,2,1:T(4,128)S(1)} %get-tuple-element.25), channel_id=1, source_target_pairs={{0,2},{1,3},{2,0},{3,1},{4,6},{5,7},{6,4},{7,5},{8,10},{9,11},{10,... | collective-permute-start | bytes 1544 | tf_op jit(solution)/shard_map/ppermute | solution.py:200
  120.0 1.9 %collective-permute-done.3 = f32[16,2,4]{0,2,1:T(4,128)S(1)} collective-permute-done((f32[16,2,4]{0,2,1:T(4,128)S(1)}, f32[16,2,4]{0,2,1:T(4,128)S(1)}, u32[]{:S(2)}, u32[]{:S(2)}) %collective-permute-start.3) | collective-permute-done | bytes 544 | tf_op jit(solution)/shard_map/ppermute | solution.py:200
  121.9 0.1 copy.43
  122.1 0.1 copy.44
  122.2 2.4 %collective-permute-start.4 = (f32[8,4,4]{0,2,1:T(4,128)S(1)}, f32[8,4,4]{0,2,1:T(4,128)S(1)}, u32[]{:S(2)}, u32[]{:S(2)}) collective-permute-start(f32[8,4,4]{0,2,1:T(4,128)S(1)} %bitcast.112), channel_id=1, source_target_pairs={{0,4},{1,5},{2,6},{3,7},{4,0},{5,1},{6,2},{7,3},{8,12},{9,13},{10,... | collective-permute-start | bytes 1544 | tf_op jit(solution)/shard_map/ppermute | solution.py:200
  124.5 5.9 %collective-permute-done.4 = f32[8,4,4]{0,2,1:T(4,128)S(1)} collective-permute-done((f32[8,4,4]{0,2,1:T(4,128)S(1)}, f32[8,4,4]{0,2,1:T(4,128)S(1)}, u32[]{:S(2)}, u32[]{:S(2)}) %collective-permute-start.4) | collective-permute-done | bytes 544 | tf_op jit(solution)/shard_map/ppermute | solution.py:200
  130.5 0.1 copy.45
  130.6 0.2 copy.46
  130.8 0.1 reshape.200
  130.9 4.7 %collective-permute-start.5 = (f32[4,8,4]{1,2,0:T(4,128)S(1)}, f32[4,8,4]{1,2,0:T(4,128)S(1)}, u32[]{:S(2)}, u32[]{:S(2)}) collective-permute-start(f32[4,8,4]{1,2,0:T(4,128)S(1)} %get-tuple-element.21), channel_id=1, source_target_pairs={{0,8},{1,9},{2,10},{3,11},{4,12},{5,13},{6,14},{7,15},{8,0},{9,1},... | collective-permute-start | bytes 1544 | tf_op jit(solution)/shard_map/ppermute | solution.py:200
  135.6 8.4 %collective-permute-done.5 = f32[4,8,4]{1,2,0:T(4,128)S(1)} collective-permute-done((f32[4,8,4]{1,2,0:T(4,128)S(1)}, f32[4,8,4]{1,2,0:T(4,128)S(1)}, u32[]{:S(2)}, u32[]{:S(2)}) %collective-permute-start.5) | collective-permute-done | bytes 544 | tf_op jit(solution)/shard_map/ppermute | solution.py:200
  144.0 0.1 reshape.201
  144.1 2.5 %collective-permute-start.6 = (f32[2,16,4]{1,2,0:T(4,128)S(1)}, f32[2,16,4]{1,2,0:T(4,128)S(1)}, u32[]{:S(2)}, u32[]{:S(2)}) collective-permute-start(f32[2,16,4]{1,2,0:T(4,128)S(1)} %get-tuple-element.23), channel_id=1, source_target_pairs={{0,16},{1,17},{2,18},{3,19},{4,20},{5,21},{6,22},{7,23},{8,24},{9,... | collective-permute-start | bytes 1544 | tf_op jit(solution)/shard_map/ppermute | solution.py:200
  146.7 2.2 %collective-permute-done.6 = f32[2,16,4]{1,2,0:T(4,128)S(1)} collective-permute-done((f32[2,16,4]{1,2,0:T(4,128)S(1)}, f32[2,16,4]{1,2,0:T(4,128)S(1)}, u32[]{:S(2)}, u32[]{:S(2)}) %collective-permute-start.6) | collective-permute-done | bytes 544 | tf_op jit(solution)/shard_map/ppermute | solution.py:200
  149.0 6.7 %collective-permute-start.7 = (f32[1,32,4]{1,2,0:T(4,128)S(1)}, f32[1,32,4]{1,2,0:T(4,128)S(1)}, u32[]{:S(2)}, u32[]{:S(2)}) collective-permute-start(f32[1,32,4]{1,2,0:T(4,128)S(1)} %get-tuple-element.27), channel_id=1, source_target_pairs={{0,32},{32,0},{1,33},{33,1},{2,34},{34,2},{3,35},{35,3},{4,36},{36... | collective-permute-start | bytes 1544 | tf_op jit(solution)/shard_map/ppermute | solution.py:202
  155.8 1.9 %collective-permute-start.1 = (bf16[96,128]{1,0:T(8,128)(2,1)S(1)}, bf16[96,128]{1,0:T(8,128)(2,1)S(1)}, u32[]{:S(2)}, u32[]{:S(2)}) collective-permute-start(bf16[96,128]{1,0:T(8,128)(2,1)S(1)} %get-tuple-element.17), channel_id=1, source_target_pairs={{0,32},{32,0},{1,33},{33,1},{2,34},{34,2},{3,35},{35,3},{4,36},{36... | collective-permute-start | bytes 73736 | tf_op jit(solution)/shard_map/ppermute | solution.py:182
  157.7 0.1 copy.50
  157.8 0.1 reshape.207
  157.9 0.8 fusion
  158.7 0.2 collective-permute-done.1
  158.8 1.5 convolution_convert_fusion
  160.4 1.6 %convert_reduce_fusion = f32[2,192,128]{2,1,0:T(8,128)S(1)} fusion(bf16[16,2,192,128]{3,2,1,0:T(8,128)(2,1)} %bitcast.52), kind=kLoop, calls=%fused_computation.1 | loop fusion | flops 1523712 | bytes 1769472 | tf_op jit(solution)/shard_map/reduce_sum | solution.py:174
  162.0 0.6 slice.60
  162.6 0.7 slice_bitcast_fusion
  (40 shorter events, 0.6 us)
Async XLA Ops:
  0.6 29.9 %copy-start = (bf16[2,128,3584]{2,1,0:T(8,128)(2,1)S(1)}, bf16[2,128,3584]{2,1,0:T(8,128)(2,1)}, u32[]{:S(2)}) copy-start(bf16[2,128,3584]{2,1,0:T(8,128)(2,1)} %param.11) | copy-start | bytes 5505028
  4.9 22.2 %copy-start.6 = (bf16[1,2,32,3,2560]{4,2,3,1,0:T(8,128)(2,1)S(1)}, bf16[1,2,32,3,2560]{4,2,3,1,0:T(8,128)(2,1)}, u32[]{:S(2)}) copy-start(bf16[1,2,32,3,2560]{4,2,3,1,0:T(8,128)(2,1)} %param.9) | copy-start | bytes 2949124
  4.9 89.1 %all-to-all-start = ((bf16[64,4,2688]{2,1,0:T(4,128)(2,1)}), bf16[64,4,2688]{2,1,0:T(4,128)(2,1)}, u32[]{:S(2)}, u32[]{:S(2)}) async-start(bf16[64,4,2688]{2,1,0:T(4,128)(2,1)} %get-tuple-element.9), calls=%async_computation | async-start | bytes 2752512 | tf_op jit(solution)/shard_map/all_to_all | solution.py:144
  28.1 4.0 %collective-permute-start = (bf16[96,2560]{1,0:T(8,128)(2,1)}, bf16[96,2560]{1,0:T(8,128)(2,1)S(1)}, u32[]{:S(2)}, u32[]{:S(2)}) collective-permute-start(bf16[96,2560]{1,0:T(8,128)(2,1)} %get-tuple-element.15), channel_id=1, source_target_pairs={{0,32},{32,0},{1,33},{33,1},{2,34},{34,2},{3,35},{35,3},{4,36},{36... | collective-permute-start | bytes 1474568 | tf_op jit(solution)/shard_map/ppermute | solution.py:148
  30.6 1.5 copy-start.5
  31.6 1.4 copy-start.3
  94.0 1.2 copy-start.1
  98.4 1.1 copy-start.2
  99.6 47.1 %copy-start.8 = (s32[1,128]{1,0:T(1,128)S(1)}, s32[1,128]{1,0:T(1,128)}, u32[]{:S(2)}) copy-start(s32[1,128]{1,0:T(1,128)} %get-tuple-element.12) | copy-start | bytes 1540
  99.6 58.3 %copy-start.7 = (bf16[128,1]{0,1:T(2,128)(2,1)S(1)}, bf16[128,1]{0,1:T(2,128)(2,1)}, u32[]{:S(2)}) copy-start(bf16[128,1]{0,1:T(2,128)(2,1)} %param.7) | copy-start | bytes 772
  99.6 59.3 %copy-start.4 = (bf16[2,2560,128]{2,1,0:T(8,128)(2,1)S(1)}, bf16[2,2560,128]{2,1,0:T(8,128)(2,1)}, u32[]{:S(2)}) copy-start(bf16[2,2560,128]{2,1,0:T(8,128)(2,1)} %param.10) | copy-start | bytes 3932164
  99.6 60.8 %all-to-all-start.1 = ((bf16[32,192,128]{2,1,0:T(8,128)(2,1)}), bf16[32,192,128]{2,1,0:T(8,128)(2,1)}, u32[]{:S(2)}, u32[]{:S(2)}) async-start(bf16[32,192,128]{2,1,0:T(8,128)(2,1)} %copy-done.2), calls=%async_computation.1 | async-start | bytes 3145728 | tf_op jit(solution)/shard_map/all_to_all | solution.py:173
  111.3 4.8 %collective-permute-start.2 = (f32[32,1,4]{0,2,1:T(4,128)S(1)}, f32[32,1,4]{0,2,1:T(4,128)S(1)}, u32[]{:S(2)}, u32[]{:S(2)}) collective-permute-start(f32[32,1,4]{0,2,1:T(4,128)S(1)} %get-tuple-element.29), channel_id=1, source_target_pairs={{0,1},{1,0},{2,3},{3,2},{4,5},{5,4},{6,7},{7,6},{8,9},{9,8},{10,11... | collective-permute-start | bytes 1544 | tf_op jit(solution)/shard_map/ppermute | solution.py:200
  116.3 5.6 %collective-permute-start.3 = (f32[16,2,4]{0,2,1:T(4,128)S(1)}, f32[16,2,4]{0,2,1:T(4,128)S(1)}, u32[]{:S(2)}, u32[]{:S(2)}) collective-permute-start(f32[16,2,4]{0,2,1:T(4,128)S(1)} %get-tuple-element.25), channel_id=1, source_target_pairs={{0,2},{1,3},{2,0},{3,1},{4,6},{5,7},{6,4},{7,5},{8,10},{9,11},{10,... | collective-permute-start | bytes 1544 | tf_op jit(solution)/shard_map/ppermute | solution.py:200
  122.2 8.3 %collective-permute-start.4 = (f32[8,4,4]{0,2,1:T(4,128)S(1)}, f32[8,4,4]{0,2,1:T(4,128)S(1)}, u32[]{:S(2)}, u32[]{:S(2)}) collective-permute-start(f32[8,4,4]{0,2,1:T(4,128)S(1)} %bitcast.112), channel_id=1, source_target_pairs={{0,4},{1,5},{2,6},{3,7},{4,0},{5,1},{6,2},{7,3},{8,12},{9,13},{10,... | collective-permute-start | bytes 1544 | tf_op jit(solution)/shard_map/ppermute | solution.py:200
  130.9 13.1 %collective-permute-start.5 = (f32[4,8,4]{1,2,0:T(4,128)S(1)}, f32[4,8,4]{1,2,0:T(4,128)S(1)}, u32[]{:S(2)}, u32[]{:S(2)}) collective-permute-start(f32[4,8,4]{1,2,0:T(4,128)S(1)} %get-tuple-element.21), channel_id=1, source_target_pairs={{0,8},{1,9},{2,10},{3,11},{4,12},{5,13},{6,14},{7,15},{8,0},{9,1},... | collective-permute-start | bytes 1544 | tf_op jit(solution)/shard_map/ppermute | solution.py:200
  144.1 4.7 %collective-permute-start.6 = (f32[2,16,4]{1,2,0:T(4,128)S(1)}, f32[2,16,4]{1,2,0:T(4,128)S(1)}, u32[]{:S(2)}, u32[]{:S(2)}) collective-permute-start(f32[2,16,4]{1,2,0:T(4,128)S(1)} %get-tuple-element.23), channel_id=1, source_target_pairs={{0,16},{1,17},{2,18},{3,19},{4,20},{5,21},{6,22},{7,23},{8,24},{9,... | collective-permute-start | bytes 1544 | tf_op jit(solution)/shard_map/ppermute | solution.py:200
  149.0 8.7 %collective-permute-start.7 = (f32[1,32,4]{1,2,0:T(4,128)S(1)}, f32[1,32,4]{1,2,0:T(4,128)S(1)}, u32[]{:S(2)}, u32[]{:S(2)}) collective-permute-start(f32[1,32,4]{1,2,0:T(4,128)S(1)} %get-tuple-element.27), channel_id=1, source_target_pairs={{0,32},{32,0},{1,33},{33,1},{2,34},{34,2},{3,35},{35,3},{4,36},{36... | collective-permute-start | bytes 1544 | tf_op jit(solution)/shard_map/ppermute | solution.py:202
  155.8 3.1 %collective-permute-start.1 = (bf16[96,128]{1,0:T(8,128)(2,1)S(1)}, bf16[96,128]{1,0:T(8,128)(2,1)S(1)}, u32[]{:S(2)}, u32[]{:S(2)}) collective-permute-start(bf16[96,128]{1,0:T(8,128)(2,1)S(1)} %get-tuple-element.17), channel_id=1, source_target_pairs={{0,32},{32,0},{1,33},{33,1},{2,34},{34,2},{3,35},{35,3},{4,36},{36... | collective-permute-start | bytes 73736 | tf_op jit(solution)/shard_map/ppermute | solution.py:182
